TPU v7x, 256 devices: a whole 4x4x8 slice. The times are simulated.
256 devices in a mesh: member: 16 (over x, z_hi), cell: 16 (over y, z_lo, core).
Axes of the slice: x: 4, y: 4, z: 8 (z_hi: 4, z_lo: 2; z = z_hi * 2 + z_lo), core: 2. Of those that a mesh axis runs over, the one named last changes fastest.
Arguments:
- latent: bfloat16 [16, 24576, 1024], P('member', 'cell'), may hold values from -6 to 6
- w_in: bfloat16 [1024, 1024], replicated, may hold values from -0.1875 to 0.1875
- w_out: bfloat16 [1024, 96], replicated, may hold values from -0.1875 to 0.1875
- target: bfloat16 [96, 24576], P(None, 'cell'), may hold values from -6 to 6
- cell_mask: int32 [24576], P('cell'), may hold values 0 or 1
Outputs:
- grad_w_in: float32 [1024, 1024], P(('member', 'cell'))
- grad_w_out: float32 [1024, 96], P(('member', 'cell'))
All inputs are finite; a program needn't handle non-finite values. No bound on the sum of `cell_mask` on one device may be relied on, other than what follows from the above.
Results may differ from a plain program's by a relative error of at most 0.0055.
Values may be sent and summed in bfloat16 or wider, within the bound.
No kernel may reach another device: no remote copies, remote signals or barrier semaphores. Data moves between devices by JAX's collectives and lax.ppermute only.
A program may use at most 64 MiB of HBM per device.

v0:
```python
import jax
import jax.numpy as jnp
from jax import lax
from jax.sharding import PartitionSpec as P


def in_blocks(x, dim, peers):
    before, after = (x.shape[:dim], x.shape[dim + 1 :])
    return jnp.moveaxis(x.reshape(*before, peers, -1, *after), dim, 0)


def summed_on_arrival(x, axis, dim):
    peers = lax.axis_size(axis)
    tiles = lax.all_to_all(in_blocks(x, dim, peers), axis, 0, 0, tiled=True)
    return jnp.sum(tiles.astype(jnp.float32), axis=0)


def sent_and_summed(x, axis, dim):
    peers = lax.axis_size(axis)
    tiles = lax.all_to_all(in_blocks(x, dim, peers), axis, 0, 0, tiled=True)
    return jnp.sum(tiles, axis=0)


def kernel_fn(diff):
    return diff / jnp.sqrt(1.0 + diff * diff)


def silu_slope(pre):
    gate = jax.nn.sigmoid(pre)
    return gate * (1.0 + pre * (1.0 - gate))


def per_device(latent, w_in, w_out, target, cell_mask):
    members = lax.axis_size("member")
    cell_count = lax.axis_size("cell")
    own_latent = latent[0]
    cells_here = own_latent.shape[0]
    scale = 1.0 / jnp.sqrt(jnp.float32(cells_here * cell_count))
    pre = jnp.dot(own_latent, w_in, preferred_element_type=jnp.float32)
    hidden = jax.nn.silu(pre).astype(jnp.bfloat16)
    fields = lax.dot_general(
        w_out, hidden, (((0,), (1,)), ((), ())), preferred_element_type=jnp.float32
    ).astype(jnp.bfloat16)
    wide = fields.astype(jnp.float32)
    values = lax.all_to_all(fields[None], "member", split_axis=2, concat_axis=0, tiled=True).astype(
        jnp.float32
    )
    sums = jnp.sum(kernel_fn(values[:, None] - values[None, :]), axis=1)
    pair = lax.all_to_all(sums, "member", split_axis=0, concat_axis=2, tiled=True)[0]
    weight = cell_mask.astype(jnp.float32) * scale / members
    own_term = kernel_fn(wide - target.astype(jnp.float32))
    grad_fields = (weight[None] * (own_term - pair / members)).astype(jnp.bfloat16)
    back = lax.dot_general(
        grad_fields, w_out, (((0,), (1,)), ((), ())), preferred_element_type=jnp.float32
    )
    grad_pre = (back * silu_slope(pre)).astype(jnp.bfloat16)
    width = w_in.shape[1]
    grad_in = lax.dot_general(
        own_latent, grad_pre, (((0,), (0,)), ((), ())), preferred_element_type=jnp.float32
    )
    grad_out = lax.dot_general(
        hidden, grad_fields, (((0,), (1,)), ((), ())), preferred_element_type=jnp.float32
    )
    partial_rows = summed_on_arrival(
        jnp.concatenate([grad_in, grad_out], axis=1).astype(jnp.bfloat16), "member", 0
    )
    owned = sent_and_summed(partial_rows, "cell", 0)
    return (owned[:, :width], owned[:, width:])


def solution(mesh):
    in_specs = (P("member", "cell", None), P(), P(), P(None, "cell"), P("cell"))
    out_specs = (P(("member", "cell"), None), P(("member", "cell"), None))
    return jax.shard_map(
        per_device, mesh=mesh, in_specs=in_specs, out_specs=out_specs, check_vma=False
    )
```

profile of v0, /device:TPU:1, one launch (start us, length us, event | category | flops | bytes accessed | tf_op | source)
XLA Modules:
  0.0 188.8 jit_solution(4087096693529205506)
XLA Ops:
  0.7 1.9 copy-done
  2.5 7.5 %multiply_convert_fusion.1 = (bf16[1536,1024]{1,0:T(8,128)(2,1)S(1)}, f32[1536,1024]{1,0:T(8,128)}) fusion(bf16[1024,1024]{1,0:T(8,128)(2,1)} %param.6, bf16[1,1536,1024]{2,1,0:T(8,128)(2,1)S(1)} %copy-done), kind=kOutput, calls=%fused_computation.6 | convolution fusion | flops 3229089792 | bytes 14680064 | tf_op jit(solution)/shard_map/dot_general | solution.py:39
  10.0 1.7 copy-done.1
  11.7 1.1 convolution_convert_fusion
  12.8 1.8 copy.23
  15.1 10.5 %reduce = bf16[1536,96]{1,0:T(8,128)(2,1)} reduce(bf16[1536,1,96]{2,1,0:T(2,128)(2,1)} %bitcast.40, bf16[]{:T(256)} %broadcast.13), dimensions={1}, to_apply=%bitcast.26.reduce_sub_computation | reduce | bytes 589826
  25.7 2.3 %reshape.32 = bf16[16,2,4608]{2,1,0:T(2,128)(2,1)} reshape(bf16[1536,96]{1,0:T(8,128)(2,1)} %reduce) | data formatting | bytes 589824
  27.9 24.5 %all_to_all.28 = bf16[16,2,4608]{2,1,0:T(2,128)(2,1)} all-to-all(bf16[16,2,4608]{2,1,0:T(2,128)(2,1)} %reshape.32), channel_id=1, replica_groups=mesh['member'=16,'cell'=16] {'member'}, dimensions={0} | all-to-all | bytes 589824 | tf_op jit(solution)/shard_map/all_to_all | solution.py:45
  52.5 4.0 %reshape.33 = bf16[1536,1,96]{2,1,0:T(2,128)(2,1)} reshape(bf16[16,2,4608]{2,1,0:T(2,128)(2,1)} %all_to_all.28) | data formatting | bytes 589824
  56.5 2.6 %bitcast_convert_fusion = f32[1,96,1536]{1,0,2:T(1,128)} fusion(bf16[1536,1,96]{2,1,0:T(2,128)(2,1)} %reshape.33), kind=kLoop, calls=%fused_computation.21 | loop fusion | flops 147456 | bytes 884736 | tf_op jit(solution)/shard_map/sub | solution.py:48
  59.1 2.3 %copy.24 = f32[16,96,96]{2,1,0:T(8,128)} copy(f32[16,96,96]{1,2,0:T(8,128)} %bitcast.39) | data formatting | bytes 1179648 | tf_op jit(solution)/shard_map/sub | solution.py:48
  61.4 5.2 %fusion.2 = f32[16,96,96]{2,1,0:T(8,128)} fusion(f32[16,96,96]{2,1,0:T(8,128)} %copy.24), kind=kLoop, calls=%fused_computation.4 | loop fusion | flops 11649024 | bytes 1179648 | tf_op jit(solution)/shard_map/reduce_sum | solution.py:48
  66.6 4.5 %all-to-all-start.1 = ((f32[16,96,96]{2,1,0:T(8,128)}), f32[16,96,96]{2,1,0:T(8,128)}, u32[]{:S(2)}, u32[]{:S(2)}) async-start(f32[16,96,96]{2,1,0:T(8,128)} %fusion.2), calls=%async_computation.1 | async-start | bytes 1572864 | tf_op jit(solution)/shard_map/all_to_all | solution.py:49
  71.1 19.8 %all-to-all-done.1 = f32[16,96,96]{2,1,0:T(8,128)} async-done(((f32[16,96,96]{2,1,0:T(8,128)}), f32[16,96,96]{2,1,0:T(8,128)}, u32[]{:S(2)}, u32[]{:S(2)}) %all-to-all-start.1) | async-done | bytes 589856 | tf_op jit(solution)/shard_map/all_to_all | solution.py:49
  90.9 1.2 multiply_bitcast_fusion
  92.1 1.3 copy.26
  93.5 2.3 %div.38 = f32[96,1536]{1,0:T(8,128)} reshape(f32[1,96,16,96]{3,2,1,0:T(8,128)} %copy.26) | data formatting | bytes 1179648 | tf_op jit(solution)/shard_map/div | solution.py:52
  95.7 1.3 multiply_convert_fusion.2
  97.8 3.2 %convolution_convert_fusion.1 = bf16[1024,96]{0,1:T(8,128)(2,1)} fusion(bf16[96,1536]{1,0:T(8,128)(2,1)S(1)} %multiply_convert_fusion.2, bf16[1536,1024]{1,0:T(8,128)(2,1)} %copy-done.1), kind=kOutput, calls=%fused_computation.16 | convolution fusion | flops 302088192 | bytes 3637248 | tf_op jit(solution)/shard_map/dot_general | solution.py:61
  101.0 1.1 copy.27
  102.1 7.8 %fusion.7 = bf16[1024,1024]{0,1:T(8,128)(2,1)} fusion(bf16[1,1536,1024]{2,1,0:T(8,128)(2,1)S(1)} %copy-done, f32[1536,1024]{1,0:T(8,128)} %get-tuple-element.3, bf16[96,1536]{1,0:T(8,128)(2,1)} %copy-done.2, bf16[1024,96]{0,1:T(8,128)(2,1)} %param.7), kind=kOutput, calls=%fused_computation.15 | convolution fusion | flops 3538419712 | bytes 12025856 | tf_op jit(solution)/shard_map/dot_general | solution.py:58
  109.9 1.8 pad_maximum_fusion
  111.7 45.2 %all_to_all.29 = bf16[16,64,1120]{2,1,0:T(8,128)(2,1)S(1)} all-to-all(bf16[16,64,1120]{2,1,0:T(8,128)(2,1)S(1)} %pad_maximum_fusion), channel_id=1, replica_groups=mesh['member'=16,'cell'=16] {'member'}, dimensions={0} | all-to-all | bytes 4587520 | tf_op jit(solution)/shard_map/all_to_all | solution.py:14
  158.0 29.6 %all_to_all.30 = f32[16,4,1120]{2,1,0:T(4,128)S(1)} all-to-all(f32[16,4,1120]{2,1,0:T(4,128)} %reshape.29), channel_id=1, replica_groups=mesh['member'=16,'cell'=16] {'cell'}, dimensions={0} | all-to-all | bytes 573440 | tf_op jit(solution)/shard_map/all_to_all | solution.py:20
  (15 shorter events, 3.6 us)
Async XLA Ops:
  0.6 1.9 %copy-start = (bf16[1,1536,1024]{2,1,0:T(8,128)(2,1)S(1)}, bf16[1,1536,1024]{2,1,0:T(8,128)(2,1)}, u32[]{:S(2)}) copy-start(bf16[1,1536,1024]{2,1,0:T(8,128)(2,1)} %param.5) | copy-start | bytes 9437188
  0.6 11.1 %copy-start.3 = (bf16[1024,96]{0,1:T(8,128)(2,1)S(1)}, bf16[1024,96]{0,1:T(8,128)(2,1)}, u32[]{:S(2)}) copy-start(bf16[1024,96]{0,1:T(8,128)(2,1)} %param.7) | copy-start | bytes 589828
  10.0 1.7 copy-start.1
  56.5 14.6 %copy-start.4 = (s32[1536]{0:T(1024)S(1)}, s32[1536]{0:T(1024)}, u32[]{:S(2)}) copy-start(s32[1536]{0:T(1024)} %param.9) | copy-start | bytes 18436
  66.6 24.3 %all-to-all-start.1 = ((f32[16,96,96]{2,1,0:T(8,128)}), f32[16,96,96]{2,1,0:T(8,128)}, u32[]{:S(2)}, u32[]{:S(2)}) async-start(f32[16,96,96]{2,1,0:T(8,128)} %fusion.2), calls=%async_computation.1 | async-start | bytes 1572864 | tf_op jit(solution)/shard_map/all_to_all | solution.py:49
  97.1 0.7 copy-start.2
where the time goes:
time: 190 us; the launch traced here: 189 us
  blocking collectives  99.3 us (52%)
  other arithmetic  23.1 us (12%)
  local copies, waits for them, and re-layouts  21.8 us (11%)
  waiting for transfers between devices  19.8 us (10%)
  matrix products  19.6 us (10%)
  starting transfers between devices  4.46 us (2%)
    all_to_all x1, blocking collectives, summed_on_arrival(): tiles = lax.all_to_all(in_blocks(x, dim, peers), axis, 0, 0, tiled=True)  45.2 us
    all_to_all x1, blocking collectives, sent_and_summed(): tiles = lax.all_to_all(in_blocks(x, dim, peers), axis, 0, 0, tiled=True)  29.6 us
    all_to_all x1, blocking collectives, per_device(): lax.all_to_all(fields[None], 'member', split_axis=2, concat_axis=0, tiled...  24.5 us
    all_to_all x1, waiting for transfers between devices, per_device(): lax.all_to_all(sums, 'member', split_axis=0, concat_axis=2, tiled=True)[0]  19.8 us
    unnamed x13, local copies, waits for them, and re-layouts  11.1 us
    unnamed x1, other arithmetic  10.5 us
    dot_general x1, matrix products, per_device(): lax.dot_general(own_latent, grad_pre, (((0,), (0,)), ((), ())), preferred...  7.77 us
    dot_general x1, matrix products, per_device(): pre = jnp.dot(own_latent, w_in, preferred_element_type=jnp.float32)  7.5 us
  transfers between devices with their start and end apart: 1, of which 1 were waited for; matrix products, arithmetic and copies ran while one was open for 0% of the time, Pallas kernels for 0%

commit v1 on v0

--- a/solution.py
+++ b/solution.py
@@ -1,7 +1,20 @@
+import functools
 import jax
 import jax.numpy as jnp
 from jax import lax
 from jax.sharding import PartitionSpec as P
+
+
+def take_notes(a0, at_axis, along_dim):
+    return jnp.concatenate(
+        lax.all_to_all(
+            jnp.stack(jnp.split(a0, lax.psum(1, "member"), axis=at_axis)), "member", 0, 0
+        ),
+        axis=along_dim,
+    )
+
+
+expand_sector = functools.partial(take_notes, at_axis=2, along_dim=0)
 
 
 def in_blocks(x, dim, peers):
@@ -42,9 +55,7 @@
         w_out, hidden, (((0,), (1,)), ((), ())), preferred_element_type=jnp.float32
     ).astype(jnp.bfloat16)
     wide = fields.astype(jnp.float32)
-    values = lax.all_to_all(fields[None], "member", split_axis=2, concat_axis=0, tiled=True).astype(
-        jnp.float32
-    )
+    values = expand_sector(fields[None]).astype(jnp.float32)
     sums = jnp.sum(kernel_fn(values[:, None] - values[None, :]), axis=1)
     pair = lax.all_to_all(sums, "member", split_axis=0, concat_axis=2, tiled=True)[0]
     weight = cell_mask.astype(jnp.float32) * scale / members

time: 190 us -> 167 us (0.88)
  other arithmetic: 23.1 us -> 8.6 us
  local copies, waits for them, and re-layouts: 21.8 us -> 12.1 us
    unnamed x1 -> x0, other arithmetic: 10.5 us -> none
    unnamed x13 -> x25, local copies, waits for them, and re-layouts: 11.1 us -> 5.29 us
    sub x1, other arithmetic: 2.6 us -> 0.07 us  [per_device(): sums = jnp.sum(kernel_fn(values[:, None] - values[None, :]), axis=1)]
    sub x1 -> x0, local copies, waits for them, and re-layouts: 2.29 us -> none  [per_device(): sums = jnp.sum(kernel_fn(values[:, None] - values[None, :]), axis=1)]
where the time goes in v1:
time: 167 us; the launch traced here: 166 us
  blocking collectives  101 us (60%)
  waiting for transfers between devices  20.6 us (12%)
  matrix products  19.5 us (12%)
  local copies, waits for them, and re-layouts  12.1 us (7%)
  other arithmetic  8.6 us (5%)
  starting transfers between devices  4.28 us (3%)
    all_to_all x1, blocking collectives, summed_on_arrival(): tiles = lax.all_to_all(in_blocks(x, dim, peers), axis, 0, 0, tiled=True)  44.6 us
    all_to_all x1, blocking collectives, sent_and_summed(): tiles = lax.all_to_all(in_blocks(x, dim, peers), axis, 0, 0, tiled=True)  29.9 us
    all_to_all x1, blocking collectives, take_notes(): lax.all_to_all(jnp.stack(jnp.split(a0, lax.psum(1, 'member'), axis=at_axi...  26 us
    all_to_all x1, waiting for transfers between devices, per_device(): lax.all_to_all(sums, 'member', split_axis=0, concat_axis=2, tiled=True)[0]  20.6 us
    dot_general x1, matrix products, per_device(): lax.dot_general(own_latent, grad_pre, (((0,), (0,)), ((), ())), preferred...  7.72 us
    dot_general x1, matrix products, per_device(): pre = jnp.dot(own_latent, w_in, preferred_element_type=jnp.float32)  7.51 us
    unnamed x25, local copies, waits for them, and re-layouts  5.29 us
    all_to_all x1, starting transfers between devices, per_device(): lax.all_to_all(sums, 'member', split_axis=0, concat_axis=2, tiled=True)[0]  4.28 us
  transfers between devices with their start and end apart: 1, of which 1 were waited for; matrix products, arithmetic and copies ran while one was open for 0% of the time, Pallas kernels for 0%

profile of v1, /device:TPU:1, one launch (start us, length us, event | category | flops | bytes accessed | tf_op | source)
XLA Modules:
  0.0 166.4 jit_solution(9355427910668691714)
XLA Ops:
  0.7 1.9 %copy-done = bf16[1,1536,1024]{2,1,0:T(8,128)(2,1)S(1)} copy-done((bf16[1,1536,1024]{2,1,0:T(8,128)(2,1)S(1)}, bf16[1,1536,1024]{2,1,0:T(8,128)(2,1)}, u32[]{:S(2)}) %copy-start) | copy-done | bytes 3145752
  2.5 7.5 %multiply_convert_fusion.1 = (bf16[1536,1024]{1,0:T(8,128)(2,1)S(1)}, f32[1536,1024]{1,0:T(8,128)}) fusion(bf16[1024,1024]{1,0:T(8,128)(2,1)} %param.6, bf16[1,1536,1024]{2,1,0:T(8,128)(2,1)S(1)} %copy-done), kind=kOutput, calls=%fused_computation.6 | convolution fusion | flops 3229089792 | bytes 14680064 | tf_op jit(solution)/shard_map/dot_general | solution.py:52
  10.0 1.7 %copy-done.1 = bf16[1536,1024]{1,0:T(8,128)(2,1)} copy-done((bf16[1536,1024]{1,0:T(8,128)(2,1)}, bf16[1536,1024]{1,0:T(8,128)(2,1)S(1)}, u32[]{:S(2)}) %copy-start.1) | copy-done | bytes 3145752
  11.7 1.1 convolution_convert_fusion
  12.9 0.1 constant_dynamic-update-slice_fusion.14
  14.0 26.0 %all_to_all.24 = bf16[16,1,96,96]{3,2,1,0:T(8,128)(2,1)S(1)} all-to-all(bf16[16,1,96,96]{3,2,1,0:T(8,128)(2,1)S(1)} %constant_dynamic-update-slice_fusion), channel_id=1, replica_groups=mesh['member'=16,'cell'=16] {'member'}, dimensions={0} | all-to-all | bytes 589824 | tf_op jit(solution)/shard_map/all_to_all | solution.py:10
  40.1 3.8 %fusion.2 = f32[16,96,96]{2,1,0:T(8,128)} fusion(f32[16,96,96]{2,1,0:T(8,128)S(1)} %bitcast_convert_fusion), kind=kLoop, calls=%fused_computation.4 | loop fusion | flops 11649024 | bytes 1179648 | tf_op jit(solution)/shard_map/reduce_sum | solution.py:59
  43.9 4.3 %all-to-all-start.1 = ((f32[16,96,96]{2,1,0:T(8,128)}), f32[16,96,96]{2,1,0:T(8,128)}, u32[]{:S(2)}, u32[]{:S(2)}) async-start(f32[16,96,96]{2,1,0:T(8,128)} %fusion.2), calls=%async_computation.1 | async-start | bytes 1572864 | tf_op jit(solution)/shard_map/all_to_all | solution.py:60
  48.2 20.6 %all-to-all-done.1 = f32[16,96,96]{2,1,0:T(8,128)} async-done(((f32[16,96,96]{2,1,0:T(8,128)}), f32[16,96,96]{2,1,0:T(8,128)}, u32[]{:S(2)}, u32[]{:S(2)}) %all-to-all-start.1) | async-done | bytes 589856 | tf_op jit(solution)/shard_map/all_to_all | solution.py:60
  68.7 1.2 multiply_bitcast_fusion
  69.9 1.3 copy.13
  71.3 2.3 %div.38 = f32[96,1536]{1,0:T(8,128)} reshape(f32[1,96,16,96]{3,2,1,0:T(8,128)} %copy.13) | data formatting | bytes 1179648 | tf_op jit(solution)/shard_map/div | solution.py:63
  73.6 1.3 multiply_convert_fusion.2
  74.9 0.7 copy-done.2
  75.6 3.2 %convolution_convert_fusion.1 = bf16[1024,96]{0,1:T(8,128)(2,1)} fusion(bf16[96,1536]{1,0:T(8,128)(2,1)S(1)} %multiply_convert_fusion.2, bf16[1536,1024]{1,0:T(8,128)(2,1)} %copy-done.1), kind=kOutput, calls=%fused_computation.16 | convolution fusion | flops 302088192 | bytes 3637248 | tf_op jit(solution)/shard_map/dot_general | solution.py:72
  78.8 1.1 copy.14
  79.9 7.7 %fusion.7 = bf16[1024,1024]{0,1:T(8,128)(2,1)} fusion(bf16[1,1536,1024]{2,1,0:T(8,128)(2,1)S(1)} %copy-done, f32[1536,1024]{1,0:T(8,128)} %get-tuple-element.3, bf16[96,1536]{1,0:T(8,128)(2,1)} %copy-done.2, bf16[1024,96]{0,1:T(8,128)(2,1)} %param.7), kind=kOutput, calls=%fused_computation.15 | convolution fusion | flops 3538419712 | bytes 12025856 | tf_op jit(solution)/shard_map/dot_general | solution.py:69
  87.6 1.8 %pad_maximum_fusion = bf16[16,64,1120]{2,1,0:T(8,128)(2,1)S(1)} fusion(bf16[16,64,96]{2,1,0:T(8,128)(2,1)S(1)} %bitcast.114, bf16[16,64,1024]{2,1,0:T(8,128)(2,1)} %bitcast.113), kind=kLoop, calls=%fused_computation.13 | loop fusion | flops 4587520 | bytes 4587520 | tf_op jit(solution)/shard_map/concatenate | solution.py:76
  89.5 44.6 %all_to_all.25 = bf16[16,64,1120]{2,1,0:T(8,128)(2,1)S(1)} all-to-all(bf16[16,64,1120]{2,1,0:T(8,128)(2,1)S(1)} %pad_maximum_fusion), channel_id=1, replica_groups=mesh['member'=16,'cell'=16] {'member'}, dimensions={0} | all-to-all | bytes 4587520 | tf_op jit(solution)/shard_map/all_to_all | solution.py:27
  134.1 0.3 convert_reduce_fusion
  134.5 0.8 reshape.26
  135.3 29.9 %all_to_all.26 = f32[16,4,1120]{2,1,0:T(4,128)S(1)} all-to-all(f32[16,4,1120]{2,1,0:T(4,128)} %reshape.26), channel_id=1, replica_groups=mesh['member'=16,'cell'=16] {'cell'}, dimensions={0} | all-to-all | bytes 573440 | tf_op jit(solution)/shard_map/all_to_all | solution.py:33
  165.2 0.6 slice.8
  165.8 0.6 slice.9
  (25 shorter events, 1.2 us)
Async XLA Ops:
  0.6 1.9 %copy-start = (bf16[1,1536,1024]{2,1,0:T(8,128)(2,1)S(1)}, bf16[1,1536,1024]{2,1,0:T(8,128)(2,1)}, u32[]{:S(2)}) copy-start(bf16[1,1536,1024]{2,1,0:T(8,128)(2,1)} %param.5) | copy-start | bytes 9437188
  0.6 11.1 %copy-start.3 = (bf16[1024,96]{0,1:T(8,128)(2,1)S(1)}, bf16[1024,96]{0,1:T(8,128)(2,1)}, u32[]{:S(2)}) copy-start(bf16[1024,96]{0,1:T(8,128)(2,1)} %param.7) | copy-start | bytes 589828
  10.0 1.7 %copy-start.1 = (bf16[1536,1024]{1,0:T(8,128)(2,1)}, bf16[1536,1024]{1,0:T(8,128)(2,1)S(1)}, u32[]{:S(2)}) copy-start(bf16[1536,1024]{1,0:T(8,128)(2,1)S(1)} %get-tuple-element.2) | copy-start | bytes 9437188
  12.8 35.3 %copy-start.4 = (s32[1536]{0:T(1024)S(1)}, s32[1536]{0:T(1024)}, u32[]{:S(2)}) copy-start(s32[1536]{0:T(1024)} %param.9) | copy-start | bytes 18436
  43.9 24.9 %all-to-all-start.1 = ((f32[16,96,96]{2,1,0:T(8,128)}), f32[16,96,96]{2,1,0:T(8,128)}, u32[]{:S(2)}, u32[]{:S(2)}) async-start(f32[16,96,96]{2,1,0:T(8,128)} %fusion.2), calls=%async_computation.1 | async-start | bytes 1572864 | tf_op jit(solution)/shard_map/all_to_all | solution.py:60
  74.9 0.7 copy-start.2
